TPU v7x, 32 devices: a whole 2x2x4 slice. The times are simulated.
32 devices in a mesh: rep: 8 (over y, x, core), shard: 4 (over z).
Axes of the slice: x: 2, y: 2, z: 4, core: 2. Of those that a mesh axis runs over, the one named last changes fastest.
Arguments:
- grads_matrix: bfloat16 [8, 4, 3, 1024, 1024], P('rep', 'shard'), may hold values from -400 to 400
- grads_vector: bfloat16 [8, 4, 5, 1024], P('rep', 'shard'), may hold values from -6 to 6
- master_matrix: float32 [3, 1024, 1024], P(None, 'shard'), may hold values from -0.1875 to 0.1875
- master_vector: float32 [5, 1024], P(None, 'shard'), may hold values from 0.5 to 1.5
- moment_matrix: float32 [3, 1024, 1024], P(None, 'shard'), may hold values from -4 to 4
- moment_vector: float32 [5, 1024], P(None, 'shard'), may hold values from -4 to 4
- second_matrix: float32 [3, 1024, 1024], P(None, 'shard'), may hold values from 0.05 to 2
- second_vector: float32 [5, 1024], P(None, 'shard'), may hold values from 0.05 to 2
Outputs:
- matrix_master: float32 [3, 1024, 1024], P(None, 'shard')
- vector_master: float32 [5, 1024], P(None, 'shard')
- matrix_moment: float32 [3, 1024, 1024], P(None, 'shard')
- vector_moment: float32 [5, 1024], P(None, 'shard')
- matrix_second: float32 [3, 1024, 1024], P(None, 'shard')
- vector_second: float32 [5, 1024], P(None, 'shard')
- matrix_weights: bfloat16 [3, 1024, 1024], replicated
- vector_weights: bfloat16 [5, 1024], replicated
All inputs are finite; a program needn't handle non-finite values.
Results may differ from a plain program's by a relative error of at most 0.005.
Values may be sent and summed in bfloat16 or wider, within the bound.
A program may use at most 128 MiB of HBM per device.

v0:
```python
import jax
import jax.numpy as jnp
from jax import lax
from jax.sharding import PartitionSpec as P

STEP = 1000
beta_first = 0.9
beta_second = 0.999
learn_rate = 0.01
decay_rate = 0.1
epsilon = 1e-08


def adam_piece(total, master, moment, second, clip, decay):
    scaled = total * clip
    moment_next = beta_first * moment + (1.0 - beta_first) * scaled
    second_next = beta_second * second + (1.0 - beta_second) * scaled * scaled
    corrected = moment_next / (1.0 - beta_first**STEP)
    spread = jnp.sqrt(second_next / (1.0 - beta_second**STEP))
    update = corrected / (spread + epsilon)
    master_next = master - learn_rate * (update + decay * master)
    return (master_next, moment_next, second_next)


def squares_of(first, second):
    return jnp.sum(first * first) + jnp.sum(second * second)


def body(
    grads_matrix,
    grads_vector,
    master_matrix,
    master_vector,
    moment_matrix,
    moment_vector,
    second_matrix,
    second_vector,
):
    local_matrix = grads_matrix[0, 0].astype(jnp.float32)
    local_vector = grads_vector[0, 0].astype(jnp.float32)
    width = local_vector.shape[1]
    count = 3 * width * width + 5 * width
    part_matrix, part_vector = (
        lax.psum_scatter(
            local_matrix.astype(jnp.bfloat16), "shard", scatter_dimension=1, tiled=True
        ).astype(jnp.float32),
        lax.psum_scatter(
            local_vector.astype(jnp.bfloat16), "shard", scatter_dimension=1, tiled=True
        ).astype(jnp.float32),
    )
    mine_matrix, mine_vector = (
        lax.psum(part_matrix.astype(jnp.bfloat16), "rep").astype(jnp.float32),
        lax.psum(part_vector.astype(jnp.bfloat16), "rep").astype(jnp.float32),
    )
    squares = lax.psum(squares_of(mine_matrix, mine_vector), "shard")
    clip = jnp.minimum(1.0, 1.0 / jnp.sqrt(squares / count + 1e-06))
    master_mat, moment_mat, second_mat = adam_piece(
        mine_matrix, master_matrix, moment_matrix, second_matrix, clip, decay_rate
    )
    master_vec, moment_vec, second_vec = adam_piece(
        mine_vector, master_vector, moment_vector, second_vector, clip, 0.0
    )
    weights_mat, weights_vec = (
        lax.all_gather(master_mat.astype(jnp.bfloat16), "shard", axis=1, tiled=True),
        lax.all_gather(master_vec.astype(jnp.bfloat16), "shard", axis=1, tiled=True),
    )
    return (
        master_mat,
        master_vec,
        moment_mat,
        moment_vec,
        second_mat,
        second_vec,
        weights_mat,
        weights_vec,
    )


def solution(mesh):
    return jax.shard_map(
        body,
        mesh=mesh,
        in_specs=(
            P("rep", "shard", None, None, None),
            P("rep", "shard", None, None),
            P(None, "shard", None),
            P(None, "shard"),
            P(None, "shard", None),
            P(None, "shard"),
            P(None, "shard", None),
            P(None, "shard"),
        ),
        out_specs=(
            P(None, "shard", None),
            P(None, "shard"),
            P(None, "shard", None),
            P(None, "shard"),
            P(None, "shard", None),
            P(None, "shard"),
            P(),
            P(),
        ),
        check_vma=False,
    )
```

profile of v0, /device:TPU:0, one launch (start us, length us, event | category | flops | bytes accessed | tf_op | source)
XLA Modules:
  0.0 356.3 jit_solution(2101009983233991101)
XLA Ops:
  7.2 0.0 reduce-scatter.3.cloned.1.call-start
  7.2 0.7 reduce-scatter.3.cloned.1.call-update
  7.9 0.0 copy-start
  7.9 0.0 reduce-scatter.5.cloned.1.call-start
  8.0 0.7 reduce-scatter.5.cloned.1.call-update
  8.7 0.0 all-reduce.2.cloned.1.call-start
  8.7 115.1 %reduce-scatter.3.cloned.1.call-done = bf16[3,256,1024]{2,1,0:T(8,128)(2,1)} async-done(((bf16[3,1024,1024]{2,1,0:T(8,128)(2,1)}), bf16[3,256,1024]{2,1,0:T(8,128)(2,1)}) %reduce-scatter.3.cloned.1.call-update) | async-done | bytes 1572880 | tf_op jit(solution)/shard_map/reduce_scatter | solution.py:44
  123.8 0.0 all-reduce.2.cloned.1.call-update
  123.8 0.0 all-gather.2.cloned.1.call-start
  123.9 21.6 %reduce-scatter.5.cloned.1.call-done = bf16[5,256]{1,0:T(8,128)(2,1)} async-done(((bf16[5,1024]{1,0:T(8,128)(2,1)}), bf16[5,256]{1,0:T(8,128)(2,1)}) %reduce-scatter.5.cloned.1.call-update) | async-done | bytes 2576 | tf_op jit(solution)/shard_map/reduce_scatter | solution.py:47
  145.4 12.0 %psum.22 = bf16[5,256]{1,0:T(8,128)(2,1)S(1)} all-reduce(bf16[5,256]{1,0:T(8,128)(2,1)} %reduce-scatter.5.cloned.1.call-done), channel_id=1, replica_groups=mesh['rep'=8,'shard'=4] {'rep'}, use_global_device_ids=true, to_apply=%region_4.0 | all-reduce | flops 1280 | bytes 5120 | tf_op jit(solution)/shard_map/psum | solution.py:53
  157.5 0.6 fusion.6
  158.1 48.1 %all-reduce.2.cloned.1.call-done = bf16[3,256,1024]{2,1,0:T(8,128)(2,1)} async-done(((bf16[3,256,1024]{2,1,0:T(8,128)(2,1)}), bf16[3,256,1024]{2,1,0:T(8,128)(2,1)}) %all-reduce.2.cloned.1.call-update) | async-done | bytes 1572880 | tf_op jit(solution)/shard_map/psum | solution.py:52
  206.2 2.8 fusion.2
  210.3 12.3 %psum.23 = f32[]{:T(128)} all-reduce(f32[]{:T(128)S(6)} %add.46), channel_id=1, replica_groups=mesh['rep'=8,'shard'=4] {'shard'}, use_global_device_ids=true, to_apply=%region_6.0 | all-reduce | flops 1 | bytes 8 | tf_op jit(solution)/shard_map/psum | solution.py:55
  223.3 0.0 copy-done
  223.4 0.0 copy-start.1
  223.4 0.0 copy-start.2
  223.4 0.0 copy-start.3
  223.4 7.5 %fusion.11 = (bf16[3,256,1024]{2,1,0:T(8,128)(2,1)}, f32[3,256,1024]{2,1,0:T(8,128)}, f32[3,256,1024]{2,1,0:T(8,128)}, f32[3,256,1024]{2,1,0:T(8,128)}) fusion(f32[3,256,1024]{2,1,0:T(8,128)S(1)} %copy-done, f32[]{:T(128)S(6)} %min.3, bf16[3,256,1024]{2,1,0:T(8,128)(2,1)} %all-reduce.2.cloned.1.call-done, f32[3,256,1024]{2,1,0:T(8,128)} %param.14, ...), kind=kLoop, calls=%fused_computation.17 | loop fusion | flops 13369344 | bytes 22020100 | tf_op jit(solution)/shard_map/convert_element_type | solution.py:64
  230.9 0.0 all-gather.2.cloned.1.call-update
  230.9 0.0 copy-done.1
  230.9 0.0 copy-done.2
  230.9 0.0 copy-done.3
  231.0 0.6 fusion.8
  231.6 13.2 %all_gather.7 = bf16[5,1024]{1,0:T(8,128)(2,1)S(1)} all-gather(bf16[5,256]{1,0:T(8,128)(2,1)S(1)} %get-tuple-element.8), channel_id=1, replica_groups=mesh['rep'=8,'shard'=4] {'shard'}, dimensions={1}, use_global_device_ids=true | all-gather | bytes 12800 | tf_op jit(solution)/shard_map/all_gather | solution.py:65
  244.8 98.1 %all-gather.2.cloned.1.call-done = bf16[3,1024,1024]{2,1,0:T(8,128)(2,1)} async-done(((bf16[3,256,1024]{2,1,0:T(8,128)(2,1)}), bf16[3,1024,1024]{2,1,0:T(8,128)(2,1)}) %all-gather.2.cloned.1.call-update) | async-done | bytes 6291472 | tf_op jit(solution)/shard_map/all_gather | solution.py:64
  342.9 6.2 %copy.19 = bf16[3,1024,1024]{2,1,0:T(8,128)(2,1)} copy(bf16[3,1024,1024]{2,1,0:T(8,128)(2,1)} %all-gather.2.cloned.1.call-done) | data formatting | bytes 12582912
  349.1 0.6 copy.20
Async XLA Ops:
  7.2 116.6 %reduce-scatter.3.cloned.1.call-start = ((), (), s32[]{:S(2)}) async-start(), calls=%async_computation.2 | async-start | bytes 7864320 | tf_op jit(solution)/shard_map/reduce_scatter | solution.py:44
  7.9 215.5 %copy-start = (f32[3,256,1024]{2,1,0:T(8,128)S(1)}, f32[3,256,1024]{2,1,0:T(8,128)}, u32[]{:S(2)}) copy-start(f32[3,256,1024]{2,1,0:T(8,128)} %param.10) | copy-start | bytes 9437188
  7.9 137.5 %reduce-scatter.5.cloned.1.call-start = ((), (), s32[]{:S(2)}) async-start(), calls=%async_computation.4 | async-start | bytes 20480 | tf_op jit(solution)/shard_map/reduce_scatter | solution.py:47
  8.7 197.5 %all-reduce.2.cloned.1.call-start = ((), (), s32[]{:S(2)}) async-start(), calls=%async_computation.3 | async-start | bytes 3145728 | tf_op jit(solution)/shard_map/psum | solution.py:52
  123.8 219.1 %all-gather.2.cloned.1.call-start = ((), (), s32[]{:S(2)}) async-start(), calls=%async_computation.5 | async-start | bytes 7864320 | tf_op jit(solution)/shard_map/all_gather | solution.py:64
  223.4 7.6 %copy-start.1 = (f32[5,256]{1,0:T(8,128)S(1)}, f32[5,256]{1,0:T(8,128)}, u32[]{:S(2)}) copy-start(f32[5,256]{1,0:T(8,128)} %param.11) | copy-start | bytes 15364
  223.4 7.6 %copy-start.2 = (f32[5,256]{1,0:T(8,128)S(1)}, f32[5,256]{1,0:T(8,128)}, u32[]{:S(2)}) copy-start(f32[5,256]{1,0:T(8,128)} %param.15) | copy-start | bytes 15364
  223.4 7.6 %copy-start.3 = (f32[5,256]{1,0:T(8,128)S(1)}, f32[5,256]{1,0:T(8,128)}, u32[]{:S(2)}) copy-start(f32[5,256]{1,0:T(8,128)} %param.13) | copy-start | bytes 15364
Sparse Core Ops, SparseCore 0:
  10.3 113.4 reduce-scatter.2
  126.0 19.3 reduce-scatter.4
  149.0 57.1 all-reduce.1
  231.0 111.8 all-gather.1
where the time goes:
time: 357 us; the launch traced here: 356 us
  waiting for transfers between devices  284 us (80%)
  blocking collectives  37.6 us (11%)
  between operations  15.8 us (4%)
  other arithmetic  11.6 us (3%)
  local copies, waits for them, and re-layouts  6.82 us (2%)
    reduce_scatter x1, waiting for transfers between devices, body(): lax.psum_scatter(local_matrix.astype(jnp.bfloat16), 'shard', scatter_dime...  115 us
    all_gather x1, waiting for transfers between devices, body(): lax.all_gather(master_mat.astype(jnp.bfloat16), 'shard', axis=1, tiled=True)  98.1 us
    psum x1, waiting for transfers between devices, body(): lax.psum(part_matrix.astype(jnp.bfloat16), 'rep').astype(jnp.float32)  48.1 us
    reduce_scatter x1, waiting for transfers between devices, body(): lax.psum_scatter(local_vector.astype(jnp.bfloat16), 'shard', scatter_dime...  21.6 us
    all_gather x1, blocking collectives, body(): lax.all_gather(master_vec.astype(jnp.bfloat16), 'shard', axis=1, tiled=True)  13.2 us
    psum x1, blocking collectives, body(): squares = lax.psum(squares_of(mine_matrix, mine_vector), 'shard')  12.3 us
    psum x1, blocking collectives, body(): lax.psum(part_vector.astype(jnp.bfloat16), 'rep').astype(jnp.float32)  12 us
    convert_element_type x1, other arithmetic, body(): master_mat.astype(jnp.bfloat16)  7.51 us
  transfers between devices with their start and end apart: 4, of which 4 were waited for; matrix products, arithmetic and copies ran while one was open for 0% of the time, Pallas kernels for 0%

commit v1 on v0

--- a/solution.py
+++ b/solution.py
@@ -9,6 +9,28 @@
 learn_rate = 0.01
 decay_rate = 0.1
 epsilon = 1e-08
+
+
+def in_order(blocks, dim):
+    blocks = jnp.moveaxis(blocks, 0, dim)
+    lengths = blocks.shape
+    return blocks.reshape(*lengths[:dim], lengths[dim] * lengths[dim + 1], *lengths[dim + 2 :])
+
+
+def grow_blocks(array, axis):
+    size = lax.axis_size(axis)
+    tiles = array[None]
+    for level in range(size.bit_length() - 1):
+        stride = 1 << level
+        partner_block = lax.ppermute(tiles, axis, [(i, i ^ stride) for i in range(size)])
+        both = jnp.stack([tiles, partner_block])
+        upper = lax.axis_index(axis) >> level & 1
+        tiles = jnp.where(upper == 0, both, both[::-1]).reshape(-1, *array.shape)
+    return tiles
+
+
+def doubled_up(x, axis, dim):
+    return in_order(grow_blocks(x, axis), dim)
 
 
 def adam_piece(total, master, moment, second, clip, decay):
@@ -62,7 +84,7 @@
     )
     weights_mat, weights_vec = (
         lax.all_gather(master_mat.astype(jnp.bfloat16), "shard", axis=1, tiled=True),
-        lax.all_gather(master_vec.astype(jnp.bfloat16), "shard", axis=1, tiled=True),
+        doubled_up(master_vec.astype(jnp.bfloat16), "shard", 1),
     )
     return (
         master_mat,

time: 357 us -> 356 us (level)
  blocking collectives: 37.6 us -> 24.4 us
  waiting for transfers between devices: 284 us -> 297 us
    all_gather x1 -> x0, blocking collectives: 13.2 us -> none  [body(): lax.all_gather(master_vec.astype(jnp.bfloat16), 'shard', axis=1, tiled=True)]
    ppermute x0 -> x2, waiting for transfers between devices: none -> 8.23 us  [grow_blocks(): lax.ppermute(tiles, axis, [(i, i ^ stride) for i in range(size)])]
    all_gather x1, waiting for transfers between devices: 98.1 us -> 102 us  [body(): lax.all_gather(master_mat.astype(jnp.bfloat16), 'shard', axis=1, tiled=True)]
  transfers between devices with their start and end apart: 4 -> 6, of which waited for: 4 -> 6; matrix products, arithmetic and copies ran while one was open for 0% -> 1% of each run, Pallas kernels for 0% -> 0%
where the time goes in v1:
time: 356 us
  waiting for transfers between devices  297 us (83%)
  blocking collectives  24.4 us (7%)
  between operations  15.9 us (4%)
  other arithmetic  11.6 us (3%)
  local copies, waits for them, and re-layouts  6.84 us (2%)
    reduce_scatter x1, waiting for transfers between devices, body(): lax.psum_scatter(local_matrix.astype(jnp.bfloat16), 'shard', scatter_dime...  115 us
    all_gather x1, waiting for transfers between devices, body(): lax.all_gather(master_mat.astype(jnp.bfloat16), 'shard', axis=1, tiled=True)  102 us
    psum x1, waiting for transfers between devices, body(): lax.psum(part_matrix.astype(jnp.bfloat16), 'rep').astype(jnp.float32)  48.1 us
    reduce_scatter x1, waiting for transfers between devices, body(): lax.psum_scatter(local_vector.astype(jnp.bfloat16), 'shard', scatter_dime...  21.6 us
    psum x1, blocking collectives, body(): squares = lax.psum(squares_of(mine_matrix, mine_vector), 'shard')  12.3 us
    psum x1, blocking collectives, body(): lax.psum(part_vector.astype(jnp.bfloat16), 'rep').astype(jnp.float32)  12 us
    ppermute x2, waiting for transfers between devices, grow_blocks(): lax.ppermute(tiles, axis, [(i, i ^ stride) for i in range(size)])  8.23 us
    convert_element_type x1, other arithmetic, body(): master_mat.astype(jnp.bfloat16)  7.51 us
  transfers between devices with their start and end apart: 6, of which 6 were waited for; matrix products, arithmetic and copies ran while one was open for 1% of the time, Pallas kernels for 0%

profile of v1, /device:TPU:0, one launch (start us, length us, event | category | flops | bytes accessed | tf_op | source)
XLA Modules:
  0.0 355.6 jit_solution(15740956770587087819)
XLA Ops:
  7.2 0.0 reduce-scatter.3.cloned.1.call-start
  7.2 0.7 reduce-scatter.3.cloned.1.call-update
  7.9 0.0 copy-start
  7.9 0.0 reduce-scatter.5.cloned.1.call-start
  8.0 0.7 reduce-scatter.5.cloned.1.call-update
  8.7 0.0 all-reduce.2.cloned.1.call-start
  8.7 115.1 %reduce-scatter.3.cloned.1.call-done = bf16[3,256,1024]{2,1,0:T(8,128)(2,1)} async-done(((bf16[3,1024,1024]{2,1,0:T(8,128)(2,1)}), bf16[3,256,1024]{2,1,0:T(8,128)(2,1)}) %reduce-scatter.3.cloned.1.call-update) | async-done | bytes 1572880 | tf_op jit(solution)/shard_map/reduce_scatter | solution.py:66
  123.8 0.0 all-reduce.2.cloned.1.call-update
  123.8 0.0 all-gather.2.cloned.1.call-start
  123.9 21.6 %reduce-scatter.5.cloned.1.call-done = bf16[5,256]{1,0:T(8,128)(2,1)} async-done(((bf16[5,1024]{1,0:T(8,128)(2,1)}), bf16[5,256]{1,0:T(8,128)(2,1)}) %reduce-scatter.5.cloned.1.call-update) | async-done | bytes 2576 | tf_op jit(solution)/shard_map/reduce_scatter | solution.py:69
  145.4 12.0 %psum.22 = bf16[5,256]{1,0:T(8,128)(2,1)S(1)} all-reduce(bf16[5,256]{1,0:T(8,128)(2,1)} %reduce-scatter.5.cloned.1.call-done), channel_id=1, replica_groups=mesh['rep'=8,'shard'=4] {'rep'}, use_global_device_ids=true, to_apply=%region_4.0 | all-reduce | flops 1280 | bytes 5120 | tf_op jit(solution)/shard_map/psum | solution.py:75
  157.5 0.6 fusion.6
  158.1 48.1 %all-reduce.2.cloned.1.call-done = bf16[3,256,1024]{2,1,0:T(8,128)(2,1)} async-done(((bf16[3,256,1024]{2,1,0:T(8,128)(2,1)}), bf16[3,256,1024]{2,1,0:T(8,128)(2,1)}) %all-reduce.2.cloned.1.call-update) | async-done | bytes 1572880 | tf_op jit(solution)/shard_map/psum | solution.py:74
  206.2 2.8 fusion.2
  210.3 12.3 %psum.23 = f32[]{:T(128)} all-reduce(f32[]{:T(128)S(6)} %add.46), channel_id=1, replica_groups=mesh['rep'=8,'shard'=4] {'shard'}, use_global_device_ids=true, to_apply=%region_6.0 | all-reduce | flops 1 | bytes 8 | tf_op jit(solution)/shard_map/psum | solution.py:77
  223.3 0.0 copy-done
  223.4 0.0 copy-start.2
  223.4 0.0 copy-start.3
  223.4 0.0 copy-start.4
  223.4 7.5 %fusion.12 = (bf16[3,256,1024]{2,1,0:T(8,128)(2,1)}, f32[3,256,1024]{2,1,0:T(8,128)}, f32[3,256,1024]{2,1,0:T(8,128)}, f32[3,256,1024]{2,1,0:T(8,128)}) fusion(f32[3,256,1024]{2,1,0:T(8,128)S(1)} %copy-done, f32[]{:T(128)S(6)} %min.3, bf16[3,256,1024]{2,1,0:T(8,128)(2,1)} %all-reduce.2.cloned.1.call-done, f32[3,256,1024]{2,1,0:T(8,128)} %param.14, ...), kind=kLoop, calls=%fused_computation.25 | loop fusion | flops 13369344 | bytes 22020100 | tf_op jit(solution)/shard_map/convert_element_type | solution.py:86
  230.9 0.0 all-gather.2.cloned.1.call-update
  230.9 0.0 copy-done.2
  230.9 0.0 copy-done.3
  231.0 0.6 convert_bitcast_fusion.1
  231.6 0.0 collective-permute-start
  231.6 3.6 %collective-permute-done = bf16[1,5,256]{2,1,0:T(8,128)(2,1)S(1)} collective-permute-done((bf16[1,5,256]{2,1,0:T(8,128)(2,1)S(1)}, bf16[1,5,256]{2,1,0:T(8,128)(2,1)S(1)}, u32[]{:S(2)}, u32[]{:S(2)}) %collective-permute-start) | collective-permute-done | bytes 2592 | tf_op jit(solution)/shard_map/ppermute | solution.py:25
  235.2 0.1 collective-permute-start.1
  235.3 4.6 %collective-permute-done.1 = bf16[2,5,256]{2,1,0:T(8,128)(2,1)S(1)} collective-permute-done((bf16[2,5,256]{2,1,0:T(8,128)(2,1)S(1)}, bf16[2,5,256]{2,1,0:T(8,128)(2,1)S(1)}, u32[]{:S(2)}, u32[]{:S(2)}) %collective-permute-start.1) | collective-permute-done | bytes 5152 | tf_op jit(solution)/shard_map/ppermute | solution.py:25
  240.0 0.6 copy.17
  240.6 102.3 %all-gather.2.cloned.1.call-done = bf16[3,1024,1024]{2,1,0:T(8,128)(2,1)} async-done(((bf16[3,256,1024]{2,1,0:T(8,128)(2,1)}), bf16[3,1024,1024]{2,1,0:T(8,128)(2,1)}) %all-gather.2.cloned.1.call-update) | async-done | bytes 6291472 | tf_op jit(solution)/shard_map/all_gather | solution.py:86
  342.9 6.2 %copy.22 = bf16[3,1024,1024]{2,1,0:T(8,128)(2,1)} copy(bf16[3,1024,1024]{2,1,0:T(8,128)(2,1)} %all-gather.2.cloned.1.call-done) | data formatting | bytes 12582912
  349.1 0.0 copy-done.1
  (8 shorter events, 0.0 us)
Async XLA Ops:
  7.2 116.6 %reduce-scatter.3.cloned.1.call-start = ((), (), s32[]{:S(2)}) async-start(), calls=%async_computation.2 | async-start | bytes 7864320 | tf_op jit(solution)/shard_map/reduce_scatter | solution.py:66
  7.9 215.5 %copy-start = (f32[3,256,1024]{2,1,0:T(8,128)S(1)}, f32[3,256,1024]{2,1,0:T(8,128)}, u32[]{:S(2)}) copy-start(f32[3,256,1024]{2,1,0:T(8,128)} %param.10) | copy-start | bytes 9437188
  7.9 137.5 %reduce-scatter.5.cloned.1.call-start = ((), (), s32[]{:S(2)}) async-start(), calls=%async_computation.4 | async-start | bytes 20480 | tf_op jit(solution)/shard_map/reduce_scatter | solution.py:69
  8.7 197.5 %all-reduce.2.cloned.1.call-start = ((), (), s32[]{:S(2)}) async-start(), calls=%async_computation.3 | async-start | bytes 3145728 | tf_op jit(solution)/shard_map/psum | solution.py:74
  123.8 219.1 %all-gather.2.cloned.1.call-start = ((), (), s32[]{:S(2)}) async-start(), calls=%async_computation.5 | async-start | bytes 7864320 | tf_op jit(solution)/shard_map/all_gather | solution.py:86
  223.4 7.6 %copy-start.2 = (f32[5,256]{1,0:T(8,128)S(1)}, f32[5,256]{1,0:T(8,128)}, u32[]{:S(2)}) copy-start(f32[5,256]{1,0:T(8,128)} %param.11) | copy-start | bytes 15364
  223.4 7.6 %copy-start.3 = (f32[5,256]{1,0:T(8,128)S(1)}, f32[5,256]{1,0:T(8,128)}, u32[]{:S(2)}) copy-start(f32[5,256]{1,0:T(8,128)} %param.15) | copy-start | bytes 15364
  223.4 7.6 %copy-start.4 = (f32[5,256]{1,0:T(8,128)S(1)}, f32[5,256]{1,0:T(8,128)}, u32[]{:S(2)}) copy-start(f32[5,256]{1,0:T(8,128)} %param.13) | copy-start | bytes 15364
  231.6 117.5 %copy-start.1 = (f32[5,256]{1,0:T(8,128)}, f32[5,256]{1,0:T(8,128)S(1)}, u32[]{:S(2)}) copy-start(f32[5,256]{1,0:T(8,128)S(1)} %get-tuple-element.27) | copy-start | bytes 15364
  231.6 3.6 %collective-permute-start = (bf16[1,5,256]{2,1,0:T(8,128)(2,1)S(1)}, bf16[1,5,256]{2,1,0:T(8,128)(2,1)S(1)}, u32[]{:S(2)}, u32[]{:S(2)}) collective-permute-start(bf16[1,5,256]{2,1,0:T(8,128)(2,1)S(1)} %convert_bitcast_fusion), channel_id=1, source_target_pairs={{0,1},{1,0},{2,3},{3,2},{4,5},{5,4},{6,7},{7,6},{8,9},{9,8},{10,11... | collective-permute-start | bytes 7688 | tf_op jit(solution)/shard_map/ppermute | solution.py:25
  235.2 4.7 %collective-permute-start.1 = (bf16[2,5,256]{2,1,0:T(8,128)(2,1)S(1)}, bf16[2,5,256]{2,1,0:T(8,128)(2,1)S(1)}, u32[]{:S(2)}, u32[]{:S(2)}) collective-permute-start(bf16[2,5,256]{2,1,0:T(8,128)(2,1)S(1)} %get-tuple-element.17), channel_id=1, source_target_pairs={{0,2},{1,3},{2,0},{3,1},{4,6},{5,7},{6,4},{7,5},{8,10},{9,11},{10,... | collective-permute-start | bytes 15368 | tf_op jit(solution)/shard_map/ppermute | solution.py:25
Sparse Core Ops, SparseCore 0:
  10.3 113.4 reduce-scatter.2
  126.0 19.3 reduce-scatter.4
  149.0 57.1 all-reduce.1
  231.0 111.7 all-gather.1
